TPU v7x, 128 devices: a whole 4x4x4 slice. The times are simulated.
128 devices in a mesh: grp: 4 (over x_hi, core), tile: 32 (over x_lo, y, z).
Axes of the slice: x: 4 (x_hi: 2, x_lo: 2; x = x_hi * 2 + x_lo), y: 4, z: 4, core: 2. Of those that a mesh axis runs over, the one named last changes fastest.
Arguments:
- start_field: float32 [512, 512, 512], P('grp', 'tile'), may hold values from -4 to 4
- class_ids: int32 [512, 512], P('tile'), may hold values from 0 to 7
- run_levels: int32 [512, 8], replicated, may hold values from 0 to 7
- steepness: float32 [512], replicated, may hold values from 0.1 to 1
- step_pick: int32 [512], replicated, may hold values from 1 to 4
- input_layer: float32 [69, 2048], replicated, may hold values from -2 to 2
- output_layer: bfloat16 [2048, 262144], P(None, ('grp', 'tile')), may hold values from -0.125 to 0.125
- output_bias: float32 [262144], P(('grp', 'tile')), may hold values from -1.5 to 1.5
Outputs:
- misfit: bfloat16 [512, 262144], P(None, ('grp', 'tile'))
- output_next: bfloat16 [2048, 262144], P(None, ('grp', 'tile'))
- bias_next: float32 [262144], P(('grp', 'tile'))
- input_next: float32 [69, 2048], replicated
All inputs are finite; a program needn't handle non-finite values.
Results may differ from a plain program's by a relative error of at most 0.0029.
The roundings to bfloat16 on the way count: a program that leaves them out, or rounds other values in their place, can miss the bound.
Values sent between devices are 32-bit elements; how exact they have to be, the bound alone decides.
A program may use at most 128 MiB of HBM per device.

v0:
```python
import jax
import jax.numpy as jnp
from jax import lax
from jax.sharding import Mesh
from jax.sharding import PartitionSpec as P

STEPS = 4
LEVELS = 8
GRP = ("grp_0", "grp_1")
GRP_TILE = ("grp_0", "grp_1", "tile")


def with_halo(value, sides, width):
    for axis, dim in sides:
        size, length = (lax.axis_size(axis), value.shape[dim])
        up = [(i, (i + 1) % size) for i in range(size - 1)]
        down = [(j, i) for i, j in up]
        last = lax.slice_in_dim(value, length - width, length, axis=dim)
        initial = lax.slice_in_dim(value, 0, width, axis=dim)
        before = lax.ppermute(last, axis, up)
        after = lax.ppermute(initial, axis, down)
        value = jnp.concatenate([before, value, after], axis=dim)
    return value


def in_blocks(value, dim, length):
    shape = value.shape
    tiles = value.reshape(*shape[:dim], length, shape[dim] // length, *shape[dim + 1 :])
    return jnp.moveaxis(tiles, dim, 0)


def in_order(tiles, dim):
    tiles = jnp.moveaxis(tiles, 0, dim)
    shape = tiles.shape
    return tiles.reshape(*shape[:dim], shape[dim] * shape[dim + 1], *shape[dim + 2 :])


def turned_blocks(tiles, axes, order):
    inside = tiles.shape[1:]
    out = tiles.reshape(*(lax.axis_size(a) for a in axes), *inside)
    for k in order:
        out = lax.all_to_all(out, axes[k], k, k, tiled=True)
    return out.reshape(-1, *inside)


def core_and_chips(value, groups, order, split_dim, concat_dim):
    length = lax.axis_size(groups[0]) * lax.axis_size(groups[1])
    tiles = in_blocks(value, split_dim, length)
    return in_order(turned_blocks(tiles, groups, order), concat_dim)


def coefficients(run_levels, class_ids):
    table = 0.03 * jnp.exp(run_levels.astype(jnp.float32) * jnp.log(jnp.float32(1.35)))
    kappa = jnp.zeros((run_levels.shape[0],) + class_ids.shape, jnp.float32)
    for klass in range(run_levels.shape[1]):
        picked = jnp.where(class_ids == klass, 1.0, 0.0).astype(jnp.float32)
        kappa = kappa + picked[None] * table[:, klass][:, None, None]
    return kappa


def advance(field, kappa, steep):
    ratio = field * field
    spread = kappa * (1.0 + steep * ratio) / (1.0 + ratio)
    fpad = jnp.pad(field, ((0, 0), (0, 0), (1, 1)))
    spad = jnp.pad(spread, ((0, 0), (0, 0), (1, 1)))
    centre = field[:, 1:-1]
    middle = spread[:, 1:-1]
    total = centre + 0.5 * (middle + spread[:, :-2]) * (field[:, :-2] - centre)
    total = total + 0.5 * (middle + spread[:, 2:]) * (field[:, 2:] - centre)
    total = total + 0.5 * (middle + spad[:, 1:-1, :-2]) * (fpad[:, 1:-1, :-2] - centre)
    total = total + 0.5 * (middle + spad[:, 1:-1, 2:]) * (fpad[:, 1:-1, 2:] - centre)
    return total


def features(run_levels, step_pick, steepness):
    count = run_levels.shape[0]
    onehot = (run_levels[:, :, None] == jnp.arange(LEVELS, dtype=jnp.int32)[None, None, :]).astype(
        jnp.float32
    )
    onehot = onehot.reshape(count, -1)
    moment = (step_pick[:, None] == jnp.arange(1, STEPS + 1, dtype=jnp.int32)[None, :]).astype(
        jnp.float32
    )
    return jnp.concatenate([onehot, moment, steepness[:, None]], axis=1)


def dsilu(pre):
    logistic = jax.nn.sigmoid(pre)
    return logistic * (1.0 + pre * (1.0 - logistic))


def on_device(
    start_field, class_ids, run_levels, steepness, step_pick, input_layer, output_layer, output_bias
):
    local_runs, rows, columns = start_field.shape
    first_run = lax.axis_index(GRP) * local_runs
    levels_here = lax.dynamic_slice_in_dim(run_levels, first_run, local_runs, 0)
    steep = lax.dynamic_slice_in_dim(steepness, first_run, local_runs, 0)[:, None, None]
    pick_here = lax.dynamic_slice_in_dim(step_pick, first_run, local_runs, 0)[:, None, None]
    snapshot = jnp.zeros_like(start_field)
    class_wide = with_halo(class_ids + 1, (("tile", 0),), STEPS)
    kappa_wide = coefficients(levels_here, class_wide - 1)
    wide = with_halo(start_field, (("tile", 1),), STEPS)
    first_row = lax.axis_index("tile") * rows - STEPS
    total_rows = rows * lax.axis_size("tile")
    span = kappa_wide.shape[1]
    for step in range(STEPS):
        margin = STEPS - step - 1
        kappa_now = kappa_wide[:, step : span - step]
        wide = advance(wide, kappa_now, steep)
        row_ids = first_row + step + 1 + jnp.arange(wide.shape[1], dtype=jnp.int32)
        inside = (row_ids >= 0) & (row_ids < total_rows)
        wide = jnp.where(inside[None, :, None], wide, 0.0)
        snapshot = jnp.where(pick_here == step + 1, wide[:, margin : margin + rows], snapshot)
    flat = snapshot.reshape(local_runs, rows * columns)
    target = core_and_chips(flat, ("grp_0", "grp_1"), (0, 1), 1, 0)
    runs_total = target.shape[0]
    feats = features(run_levels, step_pick, steepness)
    pre = jnp.dot(feats, input_layer, precision=lax.Precision.HIGHEST)
    hidden = jax.nn.silu(pre).astype(jnp.bfloat16)
    error = (
        jnp.dot(hidden, output_layer, preferred_element_type=jnp.float32)
        + output_bias[None, :]
        - target
    )
    slope = (error * (2.0 / runs_total)).astype(jnp.bfloat16)
    grad = lax.dot_general(
        hidden, slope, (((0,), (0,)), ((), ())), preferred_element_type=jnp.float32
    )
    output_next = (output_layer.astype(jnp.float32) - 0.5 * grad).astype(jnp.bfloat16)
    bias_next = output_bias - 0.5 * jnp.sum(slope.astype(jnp.float32), axis=0)
    gain_slope = dsilu(pre)
    partial_back = lax.dot_general(
        slope, output_layer, (((1,), (1,)), ((), ())), preferred_element_type=jnp.float32
    )
    partial_in = lax.dot_general(
        feats, partial_back * gain_slope, (((0,), (0,)), ((), ())), precision=lax.Precision.HIGHEST
    )
    grad_in = lax.psum(partial_in, GRP_TILE)
    input_next = input_layer - 2.0 * grad_in
    return (error.astype(jnp.bfloat16), output_next, bias_next, input_next)


def solution(mesh):
    split = Mesh(mesh.devices.reshape(2, 2, mesh.shape["tile"]), ("grp_0", "grp_1", "tile"))
    return jax.shard_map(
        on_device,
        mesh=split,
        in_specs=(
            P(GRP, "tile", None),
            P("tile", None),
            P(),
            P(),
            P(),
            P(),
            P(None, GRP_TILE),
            P(GRP_TILE),
        ),
        out_specs=(P(None, GRP_TILE), P(None, GRP_TILE), P(GRP_TILE), P()),
        check_vma=False,
    )
```

profile of v0, /device:TPU:1, one launch (start us, length us, event | category | flops | bytes accessed | tf_op | source)
XLA Modules:
  0.0 382.8 jit_solution(13823181372475220173)
XLA Ops:
  8.0 4.4 %collective-permute-start.2 = (s32[4,512]{1,0:T(4,128)S(1)}, s32[4,512]{1,0:T(4,128)S(1)}, u32[]{:S(2)}, u32[]{:S(2)}) collective-permute-start(s32[4,512]{1,0:T(4,128)S(1)} %get-tuple-element.24), channel_id=1, source_target_pairs={{0,1},{1,2},{2,3},{3,4},{4,5},{5,6},{6,7},{7,8},{8,9},{9,10},{10,1... | collective-permute-start | bytes 24584 | tf_op jit(solution)/shard_map/ppermute | solution.py:20
  13.6 2.7 fusion.90
  16.7 4.2 %collective-permute-start = (f32[128,4,512]{2,0,1:T(8,128)S(1)}, f32[128,4,512]{2,0,1:T(8,128)S(1)}, u32[]{:S(2)}, u32[]{:S(2)}) collective-permute-start(f32[128,4,512]{2,0,1:T(8,128)S(1)} %copy.34), channel_id=1, source_target_pairs={{0,1},{1,2},{2,3},{3,4},{4,5},{5,6},{6,7},{7,8},{8,9},{9,10},{10,1... | collective-permute-start | bytes 3145736 | tf_op jit(solution)/shard_map/ppermute | solution.py:20
  27.8 5.3 %copy.29 = f32[128,16,512]{0,2,1:T(8,128)} copy(f32[128,16,512]{2,1,0:T(8,128)} %param.8) | data formatting | bytes 8388608 | tf_op args[0]
  34.0 14.8 %multiply_add_fusion = f32[128,24,512]{0,2,1:T(8,128)} fusion(f32[128]{0:T(128)S(1)} %get-tuple-element.27, f32[24,512]{1,0:T(8,128)S(1)} %get-tuple-element.23, f32[128]{0:T(128)S(1)} %get-tuple-element.28, f32[24,512]{1,0:T(8,128)S(1)} %get-tuple-element.22, f32[128]{0:T(128)S(1)} %get-tuple-element.29, f32[24,512]{1,0:T(8,128)S(1)} %get-tuple-element.21, ...), kind=kLoop, calls=%fused_computation.3 | loop fusion | flops 23592960 | bytes 6688768 | tf_op jit(solution)/shard_map/add | solution.py:57
  52.0 2.7 pad_maximum_fusion
  55.4 15.7 %add_divide_fusion = f32[128,24,512]{0,2,1:T(8,128)S(1)} fusion(f32[128]{0:T(128)S(1)} %dynamic_slice.11, f32[128,4,512]{0,2,1:T(8,128)} %copy-done.3, f32[128,16,512]{0,2,1:T(8,128)S(1)} %copy-done.2, f32[128,4,512]{0,2,1:T(8,128)S(1)} %copy.28, f32[128]{0:T(128)S(1)} %copy-done.25, f32[24,512]{1,0:T(8,128)S(1)} %copy-done.9, f32[128]{0:T(128)S(1)} %copy-done.27, ...), kind=kLoop, calls=%fused_computation.2 | loop fusion | flops 36175872 | bytes 12980736 | tf_op jit(solution)/shard_map/div | solution.py:63
  71.1 11.3 %fusion.11 = (f32[128,22,512]{0,2,1:T(8,128)}, f32[128,22,512]{0,2,1:T(8,128)S(1)}) fusion(f32[128,24,512]{0,2,1:T(8,128)} %multiply_add_fusion, f32[128]{0:T(128)S(1)} %dynamic_slice.11, f32[128,24,512]{0,2,1:T(8,128)S(1)} %pad_maximum_fusion, f32[128,24,512]{0,2,1:T(8,128)S(1)} %add_divide_fusion, pred[22]{0:T(512)(128)(4,1)} %compare_and_fusion), kind=kLoop, calls=%fused_computation.20 | loop fusion | flops 38928384 | bytes 64487960 | tf_op jit(solution)/shard_map/div | solution.py:63
  82.4 16.6 %fusion.29 = (f32[128,20,512]{0,2,1:T(8,128)S(1)}, f32[128,20,512]{0,2,1:T(8,128)S(1)}) fusion(f32[128,24,512]{0,2,1:T(8,128)} %multiply_add_fusion, f32[128]{0:T(128)S(1)} %dynamic_slice.11, f32[128,22,512]{0,2,1:T(8,128)S(1)} %get-tuple-element.11, f32[128,22,512]{0,2,1:T(8,128)} %get-tuple-element.10, pred[20]{0:T(512)(128)(4,1)S(1)} %copy-done.46), kind=kLoop, calls=%fused_computation.47 | loop fusion | flops 35389440 | bytes 58721280 | tf_op jit(solution)/shard_map/div | solution.py:63
  99.1 10.9 %fusion.47 = (f32[128,18,512]{0,2,1:T(8,128)}, f32[128,18,512]{0,2,1:T(8,128)}) fusion(f32[128,24,512]{0,2,1:T(8,128)} %multiply_add_fusion, f32[128]{0:T(128)S(1)} %dynamic_slice.11, f32[128,20,512]{0,2,1:T(8,128)S(1)} %get-tuple-element.9, f32[128,20,512]{0,2,1:T(8,128)S(1)} %get-tuple-element.8, pred[18]{0:T(512)(128)(4,1)S(1)} %copy-done.45), kind=kLoop, calls=%fused_computation.74 | loop fusion | flops 31850496 | bytes 52954112 | tf_op jit(solution)/shard_map/div | solution.py:63
  110.0 21.7 %fusion.60 = f32[128,16,512]{0,2,1:T(8,128)} fusion(f32[128,18,512]{0,2,1:T(8,128)} %get-tuple-element.6, f32[128,18,512]{0,2,1:T(8,128)} %get-tuple-element.7, f32[128,22,512]{0,2,1:T(8,128)} %copy-done, f32[128,20,512]{0,2,1:T(8,128)} %copy-done.1, pred[16]{0:T(512)(128)(4,1)S(1)} %copy-done.44, pred[128]{0:T(512)(128)(4,1)S(1)} %copy-done.43, ...), kind=kLoop, calls=%fused_computation.95 | loop fusion | flops 26214400 | bytes 47186448 | tf_op jit(solution)/shard_map/jit(_where)/select_n | solution.py:114
  131.7 5.6 %copy.31 = f32[4,128,2048]{2,1,0:T(8,128)} copy(f32[4,128,2048]{1,2,0:T(8,128)} %bitcast.30) | data formatting | bytes 8388608 | tf_op jit(solution)/shard_map/transpose | solution.py:29
  137.3 5.8 %all-to-all-start = ((f32[2,2,128,2048]{3,2,1,0:T(8,128)}), f32[2,2,128,2048]{3,2,1,0:T(8,128)}, u32[]{:S(2)}, u32[]{:S(2)}) async-start(f32[2,2,128,2048]{3,2,1,0:T(8,128)} %bitcast.31), calls=%async_computation | async-start | bytes 8388608 | tf_op jit(solution)/shard_map/all_to_all | solution.py:42
  143.4 5.1 %fusion.82 = f32[512,2048]{1,0:T(8,128)} fusion(f32[69,2048]{1,0:T(8,128)S(1)} %copy-done.5, f32[512,1]{0,1:T(1,128)S(1)} %bitcast.32, f32[512,4]{0,1:T(4,128)S(1)} %compare_convert_fusion, f32[512,64]{0,1:T(8,128)S(1)} %fusion.81), kind=kOutput, calls=%fused_computation.130 | convolution fusion | flops 868291584 | bytes 4900864 | tf_op jit(solution)/shard_map/dot_general | solution.py:119
  148.5 42.2 %all-to-all-done = f32[2,2,128,2048]{3,2,1,0:T(8,128)} async-done(((f32[2,2,128,2048]{3,2,1,0:T(8,128)}), f32[2,2,128,2048]{3,2,1,0:T(8,128)}, u32[]{:S(2)}, u32[]{:S(2)}) %all-to-all-start) | async-done | bytes 4194336 | tf_op jit(solution)/shard_map/all_to_all | solution.py:42
  190.6 2.6 copy.32
  193.3 9.2 %all_to_all.10 = f32[2,2,128,2048]{3,2,0,1:T(8,128)S(1)} all-to-all(f32[2,2,128,2048]{3,2,0,1:T(8,128)S(1)} %copy.32), channel_id=1, replica_groups=mesh['grp_0'=2,'grp_1'=2,'tile'=32] {'grp_1'}, dimensions={1} | all-to-all | bytes 8388608 | tf_op jit(solution)/shard_map/all_to_all | solution.py:42
  203.0 1.7 copy-done.4
  204.7 6.1 %convert_reduce_fusion = (f32[2048]{0:T(1024)S(1)}, bf16[512,2048]{1,0:T(8,128)(2,1)}, f32[512,2048]{1,0:T(8,128)S(1)}) fusion(f32[2,2,128,2048]{3,2,1,0:T(8,128)S(1)} %copy.33, f32[2048]{0:T(1024)S(1)} %copy-done.23, bf16[2048,2048]{1,0:T(8,128)(2,1)S(1)} %bitcast.35, f32[512,2048]{1,0:T(8,128)S(1)} %copy-done.4), kind=kOutput, calls=%fused_computation.121 | convolution fusion | flops 4307548160 | bytes 23085056 | tf_op jit(solution)/shard_map/dot_general | solution.py:122
  210.8 6.1 %fusion.86 = f32[512,2048]{1,0:T(8,128)} fusion(bf16[2048,2048]{1,0:T(8,128)(2,1)S(1)} %bitcast.35, f32[512,2048]{1,0:T(8,128)S(1)} %get-tuple-element.37), kind=kOutput, calls=%fused_computation.164 | convolution fusion | flops 4297064448 | bytes 16777216 | tf_op jit(solution)/shard_map/dot_general | solution.py:133
  216.8 7.0 %fusion.74 = f32[69,2048]{1,0:T(8,128)} fusion(f32[512,2048]{1,0:T(8,128)} %fusion.86, f32[512,2048]{1,0:T(8,128)S(1)} %copy-done.4, f32[512,1]{0,1:T(1,128)S(1)} %bitcast.33, f32[512,4]{0,1:T(4,128)S(1)} %compare_convert_fusion, f32[512,64]{0,1:T(8,128)S(1)} %fusion.81), kind=kOutput, calls=%fused_computation.115 | convolution fusion | flops 876680192 | bytes 9095168 | tf_op jit(solution)/shard_map/dot_general | solution.py:136
  223.9 14.6 %subtract_convert_fusion = bf16[2048,2048]{1,0:T(8,128)(2,1)} fusion(bf16[2048,2048]{1,0:T(8,128)(2,1)} %param.14, f32[512,2048]{1,0:T(8,128)} %copy-done.47, f32[512,2048]{1,0:T(8,128)} %fusion.82), kind=kOutput, calls=%fused_computation | convolution fusion | flops 4319084544 | bytes 25165824 | tf_op jit(solution)/shard_map/dot_general | solution.py:127
  239.1 135.0 %all-reduce.10.cloned.1.call-done = f32[69,2048]{1,0:T(8,128)} async-done(((f32[69,2048]{1,0:T(8,128)}), f32[69,2048]{1,0:T(8,128)}) %all-reduce.10.cloned.1.call-update) | async-done | bytes 565264 | tf_op jit(solution)/shard_map/psum | solution.py:139
  374.0 1.9 multiply_subtract_fusion
  (132 shorter events, 14.9 us)
Async XLA Ops:
  7.2 16.4 %copy-start.22 = (s32[512,8]{0,1:T(8,128)S(1)}, s32[512,8]{0,1:T(8,128)}, u32[]{:S(2)}) copy-start(s32[512,8]{0,1:T(8,128)} %param.10) | copy-start | bytes 49156
  8.0 25.9 %collective-permute-start.2 = (s32[4,512]{1,0:T(4,128)S(1)}, s32[4,512]{1,0:T(4,128)S(1)}, u32[]{:S(2)}, u32[]{:S(2)}) collective-permute-start(s32[4,512]{1,0:T(4,128)S(1)} %get-tuple-element.24), channel_id=1, source_target_pairs={{0,1},{1,2},{2,3},{3,4},{4,5},{5,6},{6,7},{7,8},{8,9},{9,10},{10,1... | collective-permute-start | bytes 24584 | tf_op jit(solution)/shard_map/ppermute | solution.py:20
  12.3 21.6 %collective-permute-start.3 = (s32[4,512]{1,0:T(4,128)S(1)}, s32[4,512]{1,0:T(4,128)S(1)}, u32[]{:S(2)}, u32[]{:S(2)}) collective-permute-start(s32[4,512]{1,0:T(4,128)S(1)} %get-tuple-element.25), channel_id=1, source_target_pairs={{1,0},{2,1},{3,2},{4,3},{5,4},{6,5},{7,6},{8,7},{9,8},{10,9},{11,1... | collective-permute-start | bytes 24584 | tf_op jit(solution)/shard_map/ppermute | solution.py:21
  16.7 32.2 %collective-permute-start = (f32[128,4,512]{2,0,1:T(8,128)S(1)}, f32[128,4,512]{2,0,1:T(8,128)S(1)}, u32[]{:S(2)}, u32[]{:S(2)}) collective-permute-start(f32[128,4,512]{2,0,1:T(8,128)S(1)} %copy.34), channel_id=1, source_target_pairs={{0,1},{1,2},{2,3},{3,4},{4,5},{5,6},{6,7},{7,8},{8,9},{9,10},{10,1... | collective-permute-start | bytes 3145736 | tf_op jit(solution)/shard_map/ppermute | solution.py:20
  22.3 27.0 %collective-permute-start.1 = (f32[128,4,512]{2,0,1:T(8,128)}, f32[128,4,512]{2,0,1:T(8,128)}, u32[]{:S(2)}, u32[]{:S(2)}) collective-permute-start(f32[128,4,512]{2,0,1:T(8,128)} %copy.35), channel_id=1, source_target_pairs={{1,0},{2,1},{3,2},{4,3},{5,4},{6,5},{7,6},{8,7},{9,8},{10,9},{11,1... | collective-permute-start | bytes 3145736 | tf_op jit(solution)/shard_map/ppermute | solution.py:21
  23.6 25.2 %copy-start.24 = (f32[128]{0:T(128)}, f32[128]{0:T(128)S(1)}, u32[]{:S(2)}) copy-start(f32[128]{0:T(128)S(1)} %get-tuple-element.27) | copy-start | bytes 1540
  23.6 25.2 %copy-start.26 = (f32[128]{0:T(128)}, f32[128]{0:T(128)S(1)}, u32[]{:S(2)}) copy-start(f32[128]{0:T(128)S(1)} %get-tuple-element.28) | copy-start | bytes 1540
  23.6 25.2 %copy-start.28 = (f32[128]{0:T(128)}, f32[128]{0:T(128)S(1)}, u32[]{:S(2)}) copy-start(f32[128]{0:T(128)S(1)} %get-tuple-element.29) | copy-start | bytes 1540
  23.6 25.2 %copy-start.30 = (f32[128]{0:T(128)}, f32[128]{0:T(128)S(1)}, u32[]{:S(2)}) copy-start(f32[128]{0:T(128)S(1)} %get-tuple-element.30) | copy-start | bytes 1540
  23.6 25.2 %copy-start.32 = (f32[128]{0:T(128)}, f32[128]{0:T(128)S(1)}, u32[]{:S(2)}) copy-start(f32[128]{0:T(128)S(1)} %get-tuple-element.31) | copy-start | bytes 1540
  23.7 25.2 %copy-start.34 = (f32[128]{0:T(128)}, f32[128]{0:T(128)S(1)}, u32[]{:S(2)}) copy-start(f32[128]{0:T(128)S(1)} %get-tuple-element.32) | copy-start | bytes 1540
  23.7 25.2 %copy-start.36 = (f32[128]{0:T(128)}, f32[128]{0:T(128)S(1)}, u32[]{:S(2)}) copy-start(f32[128]{0:T(128)S(1)} %get-tuple-element.33) | copy-start | bytes 1540
  33.9 15.0 %copy-start.6 = (f32[24,512]{1,0:T(8,128)}, f32[24,512]{1,0:T(8,128)S(1)}, u32[]{:S(2)}) copy-start(f32[24,512]{1,0:T(8,128)S(1)} %get-tuple-element.22) | copy-start | bytes 147460
  33.9 15.0 %copy-start.8 = (f32[24,512]{1,0:T(8,128)}, f32[24,512]{1,0:T(8,128)S(1)}, u32[]{:S(2)}) copy-start(f32[24,512]{1,0:T(8,128)S(1)} %get-tuple-element.23) | copy-start | bytes 147460
  34.0 14.9 %copy-start.10 = (f32[24,512]{1,0:T(8,128)}, f32[24,512]{1,0:T(8,128)S(1)}, u32[]{:S(2)}) copy-start(f32[24,512]{1,0:T(8,128)S(1)} %get-tuple-element.16) | copy-start | bytes 147460
  34.0 14.9 %copy-start.12 = (f32[24,512]{1,0:T(8,128)}, f32[24,512]{1,0:T(8,128)S(1)}, u32[]{:S(2)}) copy-start(f32[24,512]{1,0:T(8,128)S(1)} %get-tuple-element.17) | copy-start | bytes 147460
  34.0 14.9 %copy-start.14 = (f32[24,512]{1,0:T(8,128)}, f32[24,512]{1,0:T(8,128)S(1)}, u32[]{:S(2)}) copy-start(f32[24,512]{1,0:T(8,128)S(1)} %get-tuple-element.18) | copy-start | bytes 147460
  34.0 14.9 %copy-start.16 = (f32[24,512]{1,0:T(8,128)}, f32[24,512]{1,0:T(8,128)S(1)}, u32[]{:S(2)}) copy-start(f32[24,512]{1,0:T(8,128)S(1)} %get-tuple-element.19) | copy-start | bytes 147460
  34.0 14.9 %copy-start.18 = (f32[24,512]{1,0:T(8,128)}, f32[24,512]{1,0:T(8,128)S(1)}, u32[]{:S(2)}) copy-start(f32[24,512]{1,0:T(8,128)S(1)} %get-tuple-element.20) | copy-start | bytes 147460
  34.0 14.9 %copy-start.20 = (f32[24,512]{1,0:T(8,128)}, f32[24,512]{1,0:T(8,128)S(1)}, u32[]{:S(2)}) copy-start(f32[24,512]{1,0:T(8,128)S(1)} %get-tuple-element.21) | copy-start | bytes 147460
  82.4 16.6 %copy-start = (f32[128,22,512]{0,2,1:T(8,128)}, f32[128,22,512]{0,2,1:T(8,128)S(1)}, u32[]{:S(2)}) copy-start(f32[128,22,512]{0,2,1:T(8,128)S(1)} %get-tuple-element.11) | copy-start | bytes 17301508
  82.4 16.7 %copy-start.45 = (pred[18]{0:T(512)(128)(4,1)S(1)}, pred[18]{0:T(512)(128)(4,1)}, u32[]{:S(2)}) copy-start(pred[18]{0:T(512)(128)(4,1)} %compare_and_fusion.2) | copy-start | bytes 58
  137.3 53.4 %all-to-all-start = ((f32[2,2,128,2048]{3,2,1,0:T(8,128)}), f32[2,2,128,2048]{3,2,1,0:T(8,128)}, u32[]{:S(2)}, u32[]{:S(2)}) async-start(f32[2,2,128,2048]{3,2,1,0:T(8,128)} %bitcast.31), calls=%async_computation | async-start | bytes 8388608 | tf_op jit(solution)/shard_map/all_to_all | solution.py:42
  143.0 231.0 %all-reduce.10.cloned.1.call-start = ((), (), s32[]{:S(2)}) async-start(), calls=%async_computation.2 | async-start | bytes 1179648 | tf_op jit(solution)/shard_map/psum | solution.py:139
  (32 other events, 183.6 us)
Sparse Core Ops, SparseCore 0:
  224.0 150.0 all-reduce.9
where the time goes:
time: 384 us; the launch traced here: 383 us
  waiting for transfers between devices  177 us (46%)
  other arithmetic  101 us (26%)
  matrix products  38.8 us (10%)
  local copies, waits for them, and re-layouts  24.5 us (6%)
  starting transfers between devices  17 us (4%)
  between operations  14.8 us (4%)
  blocking collectives  9.24 us (2%)
    psum x1, waiting for transfers between devices, on_device(): grad_in = lax.psum(partial_in, GRP_TILE)  135 us
    div x4, other arithmetic, advance(): spread = kappa * (1.0 + steep * ratio) / (1.0 + ratio)  54.4 us
    all_to_all x1, waiting for transfers between devices, turned_blocks(): out = lax.all_to_all(out, axes[k], k, k, tiled=True)  42.2 us
    select_n x1, other arithmetic, on_device(): jnp.where(pick_here == step + 1, wide[:, margin:margin + rows], snapshot)  21.7 us
    add x1, other arithmetic, coefficients(): kappa = kappa + picked[None] * table[:, klass][:, None, None]  14.8 us
    dot_general x1, matrix products, on_device(): lax.dot_general(hidden, slope, (((0,), (0,)), ((), ())), preferred_elemen...  14.6 us
    unnamed x103, local copies, waits for them, and re-layouts  10.4 us
    all_to_all x1, blocking collectives, turned_blocks(): out = lax.all_to_all(out, axes[k], k, k, tiled=True)  9.24 us
  transfers between devices with their start and end apart: 6, of which 2 were waited for; matrix products, arithmetic and copies ran while one was open for 13% of the time, Pallas kernels for 0%

commit v1 on v0

--- a/solution.py
+++ b/solution.py
@@ -136,7 +136,8 @@
     partial_in = lax.dot_general(
         feats, partial_back * gain_slope, (((0,), (0,)), ((), ())), precision=lax.Precision.HIGHEST
     )
-    grad_in = lax.psum(partial_in, GRP_TILE)
+    parts = lax.all_gather(partial_in, GRP_TILE, axis=0, tiled=False)
+    grad_in = parts.sum(axis=0)
     input_next = input_layer - 2.0 * grad_in
     return (error.astype(jnp.bfloat16), output_next, bias_next, input_next)
 

time: 384 us -> 677 us (1.76)
  waiting for transfers between devices: 177 us -> 448 us
  other arithmetic: 101 us -> 123 us
    all_gather x0 -> x1, waiting for transfers between devices: none -> 406 us  [on_device(): parts = lax.all_gather(partial_in, GRP_TILE, axis=0, tiled=False)]
    psum x1 -> x0, waiting for transfers between devices: 135 us -> none  [on_device(): grad_in = lax.psum(partial_in, GRP_TILE)]
    reduce_sum x0 -> x1, other arithmetic: none -> 23.3 us  [on_device(): grad_in = parts.sum(axis=0)]
  transfers between devices with their start and end apart: 6 -> 6, of which waited for: 2 -> 2; matrix products, arithmetic and copies ran while one was open for 13% -> 7% of each run, Pallas kernels for 0% -> 0%
where the time goes in v1:
time: 677 us; the launch traced here: 676 us
  waiting for transfers between devices  448 us (66%)
  other arithmetic  123 us (18%)
  matrix products  38.9 us (6%)
  local copies, waits for them, and re-layouts  24.4 us (4%)
  starting transfers between devices  18.5 us (3%)
  between operations  14.8 us (2%)
  blocking collectives  9.24 us (1%)
    all_gather x1, waiting for transfers between devices, on_device(): parts = lax.all_gather(partial_in, GRP_TILE, axis=0, tiled=False)  406 us
    div x4, other arithmetic, advance(): spread = kappa * (1.0 + steep * ratio) / (1.0 + ratio)  53.4 us
    all_to_all x1, waiting for transfers between devices, turned_blocks(): out = lax.all_to_all(out, axes[k], k, k, tiled=True)  42.1 us
    reduce_sum x1, other arithmetic, on_device(): grad_in = parts.sum(axis=0)  23.3 us
    select_n x1, other arithmetic, on_device(): jnp.where(pick_here == step + 1, wide[:, margin:margin + rows], snapshot)  21.9 us
    add x1, other arithmetic, coefficients(): kappa = kappa + picked[None] * table[:, klass][:, None, None]  14.8 us
    dot_general x1, matrix products, on_device(): lax.dot_general(hidden, slope, (((0,), (0,)), ((), ())), preferred_elemen...  14.6 us
  transfers between devices with their start and end apart: 6, of which 2 were waited for; matrix products, arithmetic and copies ran while one was open for 7% of the time, Pallas kernels for 0%

profile of v1, /device:TPU:1, one launch (start us, length us, event | category | flops | bytes accessed | tf_op | source)
XLA Modules:
  0.0 676.3 jit_solution(16900371005721694945)
XLA Ops:
  8.0 4.4 collective-permute-start.2
  13.6 2.7 fusion.93
  19.3 5.8 collective-permute-start
  29.4 5.3 copy.29
  35.6 14.8 %multiply_add_fusion = f32[128,24,512]{0,2,1:T(8,128)} fusion(f32[128]{0:T(128)S(1)} %get-tuple-element.27, f32[24,512]{1,0:T(8,128)S(1)} %get-tuple-element.23, f32[128]{0:T(128)S(1)} %get-tuple-element.28, f32[24,512]{1,0:T(8,128)S(1)} %get-tuple-element.22, f32[128]{0:T(128)S(1)} %get-tuple-element.29, f32[24,512]{1,0:T(8,128)S(1)} %get-tuple-element.21, ...), kind=kLoop, calls=%fused_computation.3 | loop fusion | flops 23592960 | bytes 6688768 | tf_op jit(solution)/shard_map/add | solution.py:57
  53.6 2.8 pad_maximum_fusion
  57.0 14.7 %add_divide_fusion = f32[128,24,512]{0,2,1:T(8,128)S(1)} fusion(f32[128]{0:T(128)S(1)} %dynamic_slice.11, f32[128,4,512]{0,2,1:T(8,128)S(1)} %copy.30, f32[128,16,512]{0,2,1:T(8,128)S(1)} %copy-done.2, f32[128,4,512]{0,2,1:T(8,128)} %copy-done.3, f32[128]{0:T(128)S(1)} %copy-done.25, f32[24,512]{1,0:T(8,128)S(1)} %copy-done.9, f32[128]{0:T(128)S(1)} %copy-done.27, ...), kind=kLoop, calls=%fused_computation.2 | loop fusion | flops 36175872 | bytes 12980736 | tf_op jit(solution)/shard_map/div | solution.py:63
  71.8 11.3 %fusion.11 = (f32[128,22,512]{0,2,1:T(8,128)}, f32[128,22,512]{0,2,1:T(8,128)S(1)}) fusion(f32[128,24,512]{0,2,1:T(8,128)} %multiply_add_fusion, f32[128]{0:T(128)S(1)} %dynamic_slice.11, f32[128,24,512]{0,2,1:T(8,128)S(1)} %pad_maximum_fusion, f32[128,24,512]{0,2,1:T(8,128)S(1)} %add_divide_fusion, pred[22]{0:T(512)(128)(4,1)} %compare_and_fusion), kind=kLoop, calls=%fused_computation.20 | loop fusion | flops 38928384 | bytes 64487960 | tf_op jit(solution)/shard_map/div | solution.py:63
  83.0 16.6 %fusion.29 = (f32[128,20,512]{0,2,1:T(8,128)S(1)}, f32[128,20,512]{0,2,1:T(8,128)S(1)}) fusion(f32[128,24,512]{0,2,1:T(8,128)} %multiply_add_fusion, f32[128]{0:T(128)S(1)} %dynamic_slice.11, f32[128,22,512]{0,2,1:T(8,128)S(1)} %get-tuple-element.11, f32[128,22,512]{0,2,1:T(8,128)} %get-tuple-element.10, pred[20]{0:T(512)(128)(4,1)S(1)} %copy-done.46), kind=kLoop, calls=%fused_computation.47 | loop fusion | flops 35389440 | bytes 58721280 | tf_op jit(solution)/shard_map/div | solution.py:63
  99.7 10.9 %fusion.47 = (f32[128,18,512]{0,2,1:T(8,128)}, f32[128,18,512]{0,2,1:T(8,128)}) fusion(f32[128,24,512]{0,2,1:T(8,128)} %multiply_add_fusion, f32[128]{0:T(128)S(1)} %dynamic_slice.11, f32[128,20,512]{0,2,1:T(8,128)S(1)} %get-tuple-element.9, f32[128,20,512]{0,2,1:T(8,128)S(1)} %get-tuple-element.8, pred[18]{0:T(512)(128)(4,1)S(1)} %copy-done.45), kind=kLoop, calls=%fused_computation.74 | loop fusion | flops 31850496 | bytes 52954112 | tf_op jit(solution)/shard_map/div | solution.py:63
  110.6 21.9 %fusion.60 = f32[128,16,512]{0,2,1:T(8,128)} fusion(f32[128,18,512]{0,2,1:T(8,128)} %get-tuple-element.6, f32[128,18,512]{0,2,1:T(8,128)} %get-tuple-element.7, f32[128,22,512]{0,2,1:T(8,128)} %copy-done, f32[128,20,512]{0,2,1:T(8,128)} %copy-done.1, pred[16]{0:T(512)(128)(4,1)S(1)} %copy-done.44, pred[128]{0:T(512)(128)(4,1)S(1)} %copy-done.43, ...), kind=kLoop, calls=%fused_computation.95 | loop fusion | flops 26214400 | bytes 47186448 | tf_op jit(solution)/shard_map/jit(_where)/select_n | solution.py:114
  132.5 5.5 copy.31
  137.9 5.7 all-to-all-start
  144.0 5.2 fusion.85
  149.2 42.1 %all-to-all-done = f32[2,2,128,2048]{3,2,1,0:T(8,128)} async-done(((f32[2,2,128,2048]{3,2,1,0:T(8,128)}), f32[2,2,128,2048]{3,2,1,0:T(8,128)}, u32[]{:S(2)}, u32[]{:S(2)}) %all-to-all-start) | async-done | bytes 4194336 | tf_op jit(solution)/shard_map/all_to_all | solution.py:42
  191.3 2.6 copy.32
  193.9 9.2 %all_to_all.10 = f32[2,2,128,2048]{3,2,0,1:T(8,128)S(1)} all-to-all(f32[2,2,128,2048]{3,2,0,1:T(8,128)S(1)} %copy.32), channel_id=1, replica_groups=mesh['grp_0'=2,'grp_1'=2,'tile'=32] {'grp_1'}, dimensions={1} | all-to-all | bytes 8388608 | tf_op jit(solution)/shard_map/all_to_all | solution.py:42
  203.7 1.7 copy-done.4
  205.3 6.1 convert_reduce_fusion
  211.4 6.1 fusion.89
  217.5 7.0 %fusion.80 = f32[1,69,2048]{2,1,0:T(8,128)} fusion(f32[512,2048]{1,0:T(8,128)} %fusion.89, f32[512,2048]{1,0:T(8,128)S(1)} %copy-done.4, f32[512,1]{0,1:T(1,128)S(1)} %bitcast.35, f32[512,4]{0,1:T(4,128)S(1)} %compare_convert_fusion, f32[512,64]{0,1:T(8,128)S(1)} %fusion.84), kind=kOutput, calls=%fused_computation.125 | convolution fusion | flops 876680192 | bytes 9095168 | tf_op jit(solution)/shard_map/dot_general | solution.py:136
  225.1 14.6 %subtract_convert_fusion = bf16[2048,2048]{1,0:T(8,128)(2,1)} fusion(bf16[2048,2048]{1,0:T(8,128)(2,1)} %param.14, f32[512,2048]{1,0:T(8,128)} %copy-done.47, f32[512,2048]{1,0:T(8,128)} %fusion.85), kind=kOutput, calls=%fused_computation | convolution fusion | flops 4319084544 | bytes 25165824 | tf_op jit(solution)/shard_map/dot_general | solution.py:127
  239.7 405.5 %all-gather.4.cloned.1.call-done = f32[128,69,2048]{2,1,0:T(8,128)} async-done(((f32[1,69,2048]{2,1,0:T(8,128)}), f32[128,69,2048]{2,1,0:T(8,128)}) %all-gather.4.cloned.1.call-update) | async-done | bytes 72351760 | tf_op jit(solution)/shard_map/all_gather | solution.py:139
  645.2 23.3 %reduce_sum.19 = f32[69,2048]{1,0:T(8,128)S(1)} reduce(f32[128,69,2048]{2,1,0:T(8,128)} %all-gather.4.cloned.1.call-done, f32[]{:T(128)} %constant.40.clone.1), dimensions={0}, to_apply=%region_1.2 | reduce | flops 17946624 | bytes 72916992 | tf_op jit(solution)/shard_map/reduce_sum | solution.py:140
  (133 shorter events, 15.9 us)
Async XLA Ops:
  7.2 21.5 %copy-start.22 = (s32[512,8]{0,1:T(8,128)S(1)}, s32[512,8]{0,1:T(8,128)}, u32[]{:S(2)}) copy-start(s32[512,8]{0,1:T(8,128)} %param.10) | copy-start | bytes 49156
  8.0 27.5 %collective-permute-start.2 = (s32[4,512]{1,0:T(4,128)S(1)}, s32[4,512]{1,0:T(4,128)S(1)}, u32[]{:S(2)}, u32[]{:S(2)}) collective-permute-start(s32[4,512]{1,0:T(4,128)S(1)} %get-tuple-element.24), channel_id=1, source_target_pairs={{0,1},{1,2},{2,3},{3,4},{4,5},{5,6},{6,7},{7,8},{8,9},{9,10},{10,1... | collective-permute-start | bytes 24584 | tf_op jit(solution)/shard_map/ppermute | solution.py:20
  12.3 23.1 %collective-permute-start.3 = (s32[4,512]{1,0:T(4,128)S(1)}, s32[4,512]{1,0:T(4,128)S(1)}, u32[]{:S(2)}, u32[]{:S(2)}) collective-permute-start(s32[4,512]{1,0:T(4,128)S(1)} %get-tuple-element.25), channel_id=1, source_target_pairs={{1,0},{2,1},{3,2},{4,3},{5,4},{6,5},{7,6},{8,7},{9,8},{10,9},{11,1... | collective-permute-start | bytes 24584 | tf_op jit(solution)/shard_map/ppermute | solution.py:21
  16.7 33.8 %collective-permute-start.1 = (f32[128,4,512]{2,0,1:T(8,128)S(1)}, f32[128,4,512]{2,0,1:T(8,128)S(1)}, u32[]{:S(2)}, u32[]{:S(2)}) collective-permute-start(f32[128,4,512]{2,0,1:T(8,128)S(1)} %copy.35), channel_id=1, source_target_pairs={{1,0},{2,1},{3,2},{4,3},{5,4},{6,5},{7,6},{8,7},{9,8},{10,9},{11,1... | collective-permute-start | bytes 3145736 | tf_op jit(solution)/shard_map/ppermute | solution.py:21
  19.3 31.6 %collective-permute-start = (f32[128,4,512]{2,0,1:T(8,128)}, f32[128,4,512]{2,0,1:T(8,128)}, u32[]{:S(2)}, u32[]{:S(2)}) collective-permute-start(f32[128,4,512]{2,0,1:T(8,128)} %copy.34), channel_id=1, source_target_pairs={{0,1},{1,2},{2,3},{3,4},{4,5},{5,6},{6,7},{7,8},{8,9},{9,10},{10,1... | collective-permute-start | bytes 3145736 | tf_op jit(solution)/shard_map/ppermute | solution.py:20
  28.7 21.7 %copy-start.24 = (f32[128]{0:T(128)}, f32[128]{0:T(128)S(1)}, u32[]{:S(2)}) copy-start(f32[128]{0:T(128)S(1)} %get-tuple-element.27) | copy-start | bytes 1540
  28.7 21.7 %copy-start.26 = (f32[128]{0:T(128)}, f32[128]{0:T(128)S(1)}, u32[]{:S(2)}) copy-start(f32[128]{0:T(128)S(1)} %get-tuple-element.28) | copy-start | bytes 1540
  28.7 21.7 %copy-start.28 = (f32[128]{0:T(128)}, f32[128]{0:T(128)S(1)}, u32[]{:S(2)}) copy-start(f32[128]{0:T(128)S(1)} %get-tuple-element.29) | copy-start | bytes 1540
  28.8 21.7 %copy-start.30 = (f32[128]{0:T(128)}, f32[128]{0:T(128)S(1)}, u32[]{:S(2)}) copy-start(f32[128]{0:T(128)S(1)} %get-tuple-element.30) | copy-start | bytes 1540
  28.8 21.7 %copy-start.32 = (f32[128]{0:T(128)}, f32[128]{0:T(128)S(1)}, u32[]{:S(2)}) copy-start(f32[128]{0:T(128)S(1)} %get-tuple-element.31) | copy-start | bytes 1540
  28.8 21.7 %copy-start.34 = (f32[128]{0:T(128)}, f32[128]{0:T(128)S(1)}, u32[]{:S(2)}) copy-start(f32[128]{0:T(128)S(1)} %get-tuple-element.32) | copy-start | bytes 1540
  28.8 21.7 %copy-start.36 = (f32[128]{0:T(128)}, f32[128]{0:T(128)S(1)}, u32[]{:S(2)}) copy-start(f32[128]{0:T(128)S(1)} %get-tuple-element.33) | copy-start | bytes 1540
  35.5 15.0 %copy-start.6 = (f32[24,512]{1,0:T(8,128)}, f32[24,512]{1,0:T(8,128)S(1)}, u32[]{:S(2)}) copy-start(f32[24,512]{1,0:T(8,128)S(1)} %get-tuple-element.22) | copy-start | bytes 147460
  35.5 15.0 %copy-start.8 = (f32[24,512]{1,0:T(8,128)}, f32[24,512]{1,0:T(8,128)S(1)}, u32[]{:S(2)}) copy-start(f32[24,512]{1,0:T(8,128)S(1)} %get-tuple-element.23) | copy-start | bytes 147460
  35.6 14.9 %copy-start.10 = (f32[24,512]{1,0:T(8,128)}, f32[24,512]{1,0:T(8,128)S(1)}, u32[]{:S(2)}) copy-start(f32[24,512]{1,0:T(8,128)S(1)} %get-tuple-element.16) | copy-start | bytes 147460
  35.6 14.9 %copy-start.12 = (f32[24,512]{1,0:T(8,128)}, f32[24,512]{1,0:T(8,128)S(1)}, u32[]{:S(2)}) copy-start(f32[24,512]{1,0:T(8,128)S(1)} %get-tuple-element.17) | copy-start | bytes 147460
  35.6 14.9 %copy-start.14 = (f32[24,512]{1,0:T(8,128)}, f32[24,512]{1,0:T(8,128)S(1)}, u32[]{:S(2)}) copy-start(f32[24,512]{1,0:T(8,128)S(1)} %get-tuple-element.18) | copy-start | bytes 147460
  35.6 14.9 %copy-start.16 = (f32[24,512]{1,0:T(8,128)}, f32[24,512]{1,0:T(8,128)S(1)}, u32[]{:S(2)}) copy-start(f32[24,512]{1,0:T(8,128)S(1)} %get-tuple-element.19) | copy-start | bytes 147460
  35.6 14.9 %copy-start.18 = (f32[24,512]{1,0:T(8,128)}, f32[24,512]{1,0:T(8,128)S(1)}, u32[]{:S(2)}) copy-start(f32[24,512]{1,0:T(8,128)S(1)} %get-tuple-element.20) | copy-start | bytes 147460
  35.6 14.9 %copy-start.20 = (f32[24,512]{1,0:T(8,128)}, f32[24,512]{1,0:T(8,128)S(1)}, u32[]{:S(2)}) copy-start(f32[24,512]{1,0:T(8,128)S(1)} %get-tuple-element.21) | copy-start | bytes 147460
  83.0 16.6 %copy-start = (f32[128,22,512]{0,2,1:T(8,128)}, f32[128,22,512]{0,2,1:T(8,128)S(1)}, u32[]{:S(2)}) copy-start(f32[128,22,512]{0,2,1:T(8,128)S(1)} %get-tuple-element.11) | copy-start | bytes 17301508
  83.0 16.6 %copy-start.45 = (pred[18]{0:T(512)(128)(4,1)S(1)}, pred[18]{0:T(512)(128)(4,1)}, u32[]{:S(2)}) copy-start(pred[18]{0:T(512)(128)(4,1)} %compare_and_fusion.2) | copy-start | bytes 58
  137.9 53.3 %all-to-all-start = ((f32[2,2,128,2048]{3,2,1,0:T(8,128)}), f32[2,2,128,2048]{3,2,1,0:T(8,128)}, u32[]{:S(2)}, u32[]{:S(2)}) async-start(f32[2,2,128,2048]{3,2,1,0:T(8,128)} %bitcast.33), calls=%async_computation | async-start | bytes 8388608 | tf_op jit(solution)/shard_map/all_to_all | solution.py:42
  143.7 501.5 %all-gather.4.cloned.1.call-start = ((), (), s32[]{:S(2)}) async-start(), calls=%async_computation.2 | async-start | bytes 76087296 | tf_op jit(solution)/shard_map/all_gather | solution.py:139
  (32 other events, 183.5 us)
Sparse Core Ops, SparseCore 0:
  224.6 420.5 all-gather.3
